TPU v7x, 32 devices: a whole 2x2x4 slice. The times are simulated.
32 devices in a mesh: groups: 2 (over y), adapter: 8 (over z, x), tensor: 2 (over core).
Axes of the slice: x: 2, y: 2, z: 4, core: 2. Of those that a mesh axis runs over, the one named last changes fastest.
Arguments:
- hidden: bfloat16 [2048, 8192], P(('groups', 'adapter'), 'tensor'), parts along dimension 0, may hold values from -6 to 6
- row_adapter_index: int32 [2048, 1], P(('groups', 'adapter')), parts along dimension 0, may hold values from 0 to 7; in each aligned block of 128 rows (0 to 127, 128 to 255, ...) at most 32 rows name the same one
- adapter_shrink_weight: bfloat16 [8, 8192, 128], P('adapter', 'tensor'), may hold values from -0.0625 to 0.0625
- adapter_expand_weight: bfloat16 [8, 2, 64, 1024], P('adapter', None, None, 'tensor'), may hold values from -0.75 to 0.75
- base_partial_sums: bfloat16 [2, 2048, 2, 1024], P('tensor', ('groups', 'adapter')), parts along dimension 1, may hold values from -4 to 4
Outputs:
- kv_out: bfloat16 [2048, 2, 1024], P(('groups', 'adapter'), None, 'tensor'), parts along dimension 0
There are 2 independent parts, one for each index of `groups`. A program takes and returns all parts, laid end to end along the dimension named above; an argument that names none is the same for every part. Nothing has to cross between parts.
Inputs may be any that keep to these rules, and one draw needn't show every extreme that they name: `row_adapter_index`: within each aligned block of 128 rows (the rows of one device) no adapter is named by more than 32 rows, and this bound is reached.
All inputs are finite; a program needn't handle non-finite values.
Results may differ from a plain program's by a relative error of at most 0.006.
Values may be sent and summed in bfloat16 or wider, within the bound.
A program may use at most 64 MiB of HBM per device.

v0:
```python
import jax
import jax.numpy as jnp
from jax import lax
from jax.sharding import PartitionSpec as P


def local(
    hidden, row_adapter_index, adapter_shrink_weight, adapter_expand_weight, base_partial_sums
):
    row_count = hidden.shape[0]
    owner_count = lax.axis_size("adapter")
    capacity = max(2, (2 * row_count + owner_count - 1) // owner_count)
    slot_count = owner_count * capacity
    row_owner = row_adapter_index[:, 0]
    owner_hot = (row_owner[:, None] == jnp.arange(owner_count, dtype=jnp.int32)[None, :]).astype(
        jnp.float32
    )
    earlier = (jnp.arange(row_count)[:, None] > jnp.arange(row_count)[None, :]).astype(jnp.float32)
    before = jnp.dot(earlier, owner_hot, precision=lax.Precision.HIGHEST)
    slot_index = jnp.sum(before * owner_hot, axis=1)
    slot_hot = (slot_index[:, None] == jnp.arange(capacity, dtype=jnp.float32)[None, :]).astype(
        jnp.float32
    )
    placing = (owner_hot[:, :, None] * slot_hot[:, None, :]).reshape(row_count, slot_count)
    outgoing = jnp.dot(placing.T.astype(jnp.bfloat16), hidden, preferred_element_type=jnp.float32)
    outgoing = outgoing.astype(jnp.bfloat16).reshape(owner_count, capacity, hidden.shape[1])
    shrink_factor_table = adapter_shrink_weight[0]
    rank_index = adapter_expand_weight.shape[2]
    expand_factor_table = adapter_expand_weight[0].astype(jnp.float32)
    shrunk = lax.psum(
        jnp.einsum(
            "ocw,wk->ock",
            lax.all_to_all(outgoing, "adapter", split_axis=0, concat_axis=0, tiled=True),
            shrink_factor_table,
            preferred_element_type=jnp.float32,
        ),
        "tensor",
    )
    shrunk = shrunk.reshape(shrunk.shape[0], shrunk.shape[1], 2, rank_index)
    delta = jnp.einsum(
        "ocjk,jkf->ocjf", shrunk, expand_factor_table, precision=lax.Precision.HIGHEST
    )
    returned = lax.all_to_all(delta, "adapter", split_axis=0, concat_axis=0, tiled=True)
    row_delta = jnp.einsum(
        "rs,sjf->rjf",
        placing,
        returned.reshape(slot_count, 2, returned.shape[3]),
        precision=lax.Precision.HIGHEST,
    )
    base_sum = lax.psum_scatter(
        base_partial_sums[0].astype(jnp.float32).astype(jnp.bfloat16),
        "tensor",
        scatter_dimension=2,
        tiled=True,
    ).astype(jnp.float32)
    return (base_sum + row_delta).astype(jnp.bfloat16)


def solution(mesh):
    in_specs = (
        P(("groups", "adapter"), "tensor"),
        P(("groups", "adapter"), None),
        P("adapter", "tensor", None),
        P("adapter", None, None, "tensor"),
        P("tensor", ("groups", "adapter"), None, None),
    )
    out_specs = P(("groups", "adapter"), None, "tensor")
    return jax.shard_map(local, mesh=mesh, in_specs=in_specs, out_specs=out_specs, check_vma=False)
```

profile of v0, /device:TPU:0, one launch (start us, length us, event | category | flops | bytes accessed | tf_op | source)
XLA Modules:
  0.0 127.4 jit_solution(16831164982821652225)
XLA Ops:
  6.5 0.0 copy-start
  6.5 0.0 all-reduce.2.cloned.1.call-start
  6.5 0.9 fusion.2
  7.4 0.7 fusion.10
  8.2 0.0 copy-done
  8.2 0.7 convolution_convert_fusion
  8.9 0.0 copy-start.1
  8.9 55.4 %all_to_all.10 = bf16[8,32,4096]{2,1,0:T(8,128)(2,1)S(1)} all-to-all(bf16[8,32,4096]{2,1,0:T(8,128)(2,1)S(1)} %bitcast.34), channel_id=1, replica_groups=mesh['groups'=2,'adapter'=8,'tensor'=2] {'adapter'}, dimensions={0} | all-to-all | bytes 4194304 | tf_op jit(solution)/shard_map/all_to_all | solution.py:33
  64.3 0.0 copy-done.1
  64.3 0.0 copy-start.3
  64.3 0.7 fusion.3
  65.0 0.0 copy-start.2
  65.0 0.9 reshape.54
  65.9 0.0 all-reduce.2.cloned.1.call-update
  65.9 17.4 %all-reduce.2.cloned.1.call-done = f32[8,32,2,64]{3,2,1,0:T(2,128)} async-done(((f32[8,32,2,64]{3,2,1,0:T(2,128)}), f32[8,32,2,64]{3,2,1,0:T(2,128)}) %all-reduce.2.cloned.1.call-update) | async-done | bytes 131088 | tf_op jit(solution)/shard_map/psum | solution.py:30
  83.4 0.0 copy-done.3
  83.4 2.5 %convolution_bitcast_fusion = f32[8,32,2,512]{3,1,2,0:T(8,128)} fusion(f32[8,32,2,64]{3,2,1,0:T(2,128)} %all-reduce.2.cloned.1.call-done, bf16[1,2,64,512]{3,2,1,0:T(8,128)(2,1)S(1)} %copy-done.3), kind=kOutput, calls=%fused_computation.1 | convolution fusion | flops 201326592 | bytes 1310720 | tf_op jit(solution)/shard_map/ocjk,jkf->ocjf/dot_general | solution.py:40
  85.9 5.8 %all-to-all-start.1 = ((f32[8,32,2,512]{3,1,2,0:T(8,128)}), f32[8,32,2,512]{3,1,2,0:T(8,128)S(1)}, u32[]{:S(2)}, u32[]{:S(2)}) async-start(f32[8,32,2,512]{3,1,2,0:T(8,128)} %convolution_bitcast_fusion), calls=%async_computation.2 | async-start | bytes 2097152 | tf_op jit(solution)/shard_map/all_to_all | solution.py:43
  91.6 0.0 reduce-scatter.2.cloned.1.call-start
  91.7 0.0 copy-done.2
  91.7 0.9 copy.16
  92.6 0.0 reduce-scatter.2.cloned.1.call-update
  92.6 11.5 %reduce-scatter.2.cloned.1.call-done = bf16[128,2,512]{2,0,1:T(8,128)(2,1)} async-done(((bf16[128,2,1024]{2,0,1:T(8,128)(2,1)}), bf16[128,2,512]{2,0,1:T(8,128)(2,1)}) %reduce-scatter.2.cloned.1.call-update) | async-done | bytes 262160 | tf_op jit(solution)/shard_map/reduce_scatter | solution.py:50
  104.2 13.7 %all-to-all-done.1 = f32[8,32,2,512]{3,1,2,0:T(8,128)S(1)} async-done(((f32[8,32,2,512]{3,1,2,0:T(8,128)}), f32[8,32,2,512]{3,1,2,0:T(8,128)S(1)}, u32[]{:S(2)}, u32[]{:S(2)}) %all-to-all-start.1) | async-done | bytes 1048608 | tf_op jit(solution)/shard_map/all_to_all | solution.py:43
  117.9 1.7 %fusion.1 = bf16[128,2,512]{2,0,1:T(8,128)(2,1)S(1)} fusion(f32[8,32,2,512]{3,1,2,0:T(8,128)S(1)} %all-to-all-done.1, bf16[128,2,512]{2,0,1:T(8,128)(2,1)} %reduce-scatter.2.cloned.1.call-done, f32[128,32]{0,1:T(8,128)S(1)} %fusion.9, f32[128,8]{0,1:T(8,128)S(1)} %fusion.10), kind=kOutput, calls=%fused_computation.4 | convolution fusion | flops 403079168 | bytes 1593344 | tf_op jit(solution)/shard_map/rs,sjf->rjf/dot_general | solution.py:44
  119.5 1.0 copy.10
  (2 shorter events, 0.0 us)
Async XLA Ops:
  6.5 1.6 %copy-start = (bf16[128,4096]{1,0:T(8,128)(2,1)S(1)}, bf16[128,4096]{1,0:T(8,128)(2,1)}, u32[]{:S(2)}) copy-start(bf16[128,4096]{1,0:T(8,128)(2,1)} %param.5) | copy-start | bytes 3145732
  6.5 76.9 %all-reduce.2.cloned.1.call-start = ((), (), s32[]{:S(2)}) async-start(), calls=%async_computation.4 | async-start | bytes 524288 | tf_op jit(solution)/shard_map/psum | solution.py:30
  8.9 55.4 %copy-start.1 = (bf16[1,4096,128]{2,1,0:T(8,128)(2,1)S(1)}, bf16[1,4096,128]{2,1,0:T(8,128)(2,1)}, u32[]{:S(2)}) copy-start(bf16[1,4096,128]{2,1,0:T(8,128)(2,1)} %param.7) | copy-start | bytes 3145732
  64.3 19.1 %copy-start.3 = (bf16[1,2,64,512]{3,2,1,0:T(8,128)(2,1)S(1)}, bf16[1,2,64,512]{3,2,1,0:T(8,128)(2,1)}, u32[]{:S(2)}) copy-start(bf16[1,2,64,512]{3,2,1,0:T(8,128)(2,1)} %param.8) | copy-start | bytes 393220
  65.0 26.7 %copy-start.2 = (bf16[1,128,2,1024]{3,2,1,0:T(2,128)(2,1)S(1)}, bf16[1,128,2,1024]{3,2,1,0:T(2,128)(2,1)}, u32[]{:S(2)}) copy-start(bf16[1,128,2,1024]{3,2,1,0:T(2,128)(2,1)} %param.9) | copy-start | bytes 1572868
  85.9 32.0 %all-to-all-start.1 = ((f32[8,32,2,512]{3,1,2,0:T(8,128)}), f32[8,32,2,512]{3,1,2,0:T(8,128)S(1)}, u32[]{:S(2)}, u32[]{:S(2)}) async-start(f32[8,32,2,512]{3,1,2,0:T(8,128)} %convolution_bitcast_fusion), calls=%async_computation.2 | async-start | bytes 2097152 | tf_op jit(solution)/shard_map/all_to_all | solution.py:43
  91.6 12.5 %reduce-scatter.2.cloned.1.call-start = ((), (), s32[]{:S(2)}) async-start(), calls=%async_computation.3 | async-start | bytes 786432 | tf_op jit(solution)/shard_map/reduce_scatter | solution.py:50
Sparse Core Ops, SparseCore 0:
  66.1 17.2 all-reduce.1
  94.8 9.3 reduce-scatter.1
where the time goes:
time: 128 us; the launch traced here: 127 us
  blocking collectives  55.4 us (43%)
  waiting for transfers between devices  42.7 us (33%)
  between operations  13.5 us (11%)
  matrix products  6.45 us (5%)
  starting transfers between devices  5.8 us (5%)
  local copies, waits for them, and re-layouts  2.82 us (2%)
    all_to_all x1, blocking collectives, local(): lax.all_to_all(outgoing, 'adapter', split_axis=0, concat_axis=0, tiled=True)  55.4 us
    psum x1, waiting for transfers between devices, local(): lax.psum(jnp.einsum('ocw,wk->ock', lax.all_to_all(outgoing, 'adapter', sp...  17.4 us
    all_to_all x1, waiting for transfers between devices, local(): lax.all_to_all(delta, 'adapter', split_axis=0, concat_axis=0, tiled=True)  13.7 us
    reduce_scatter x1, waiting for transfers between devices, local(): lax.psum_scatter(base_partial_sums[0].astype(jnp.float32).astype(jnp.bflo...  11.5 us
    all_to_all x1, starting transfers between devices, local(): lax.all_to_all(delta, 'adapter', split_axis=0, concat_axis=0, tiled=True)  5.76 us
  transfers between devices with their start and end apart: 3, of which 3 were waited for; matrix products, arithmetic and copies ran while one was open for 1% of the time, Pallas kernels for 0%

commit v1 on v0

--- a/solution.py
+++ b/solution.py
@@ -1,7 +1,285 @@
+import functools
+
 import jax
 import jax.numpy as jnp
 from jax import lax
+from jax.experimental import pallas as pl
+from jax.experimental.pallas import tpu as pltpu
 from jax.sharding import PartitionSpec as P
+
+MESH = pl.DeviceIdType.MESH
+
+
+def plane_kernel(
+    nz, hidden_ref, idx_ref, w_ref, e_ref, base_ref, delta_ref, peer_base_ref,
+    hbuf, mbuf, wbuf, ebuf, acc, pbuf, rbuf,
+    hs, hr, ms, mr, wxs, wxr, wzs, wzr, ezs, ezr, eps, epr, ps, pr, bs, br, ls,
+):
+    y = lax.axis_index("groups")
+    a = lax.axis_index("adapter")
+    t = lax.axis_index("tensor")
+    z = a // 2
+    x = a % 2
+    rows = hidden_ref.shape[0]
+    chunk = hidden_ref.shape[1] // 4
+    rank = e_ref.shape[2]
+    feats = e_ref.shape[3]
+    width = w_ref.shape[2]
+
+    def coords(d):
+        return (1 - x if d // 2 else x), (1 - y if d % 2 else y)
+
+    def device(d, other=0):
+        xx, yy = coords(d)
+        return {"groups": yy, "adapter": 2 * z + xx, "tensor": 1 - t if other else t}
+
+    def along(step):
+        return {"groups": y, "adapter": 2 * (z + step) + x, "tensor": t}
+
+    def quarter(d):
+        xx, yy = coords(d)
+        return pl.ds(pl.multiple_of((2 * xx + yy) * chunk, chunk), chunk)
+
+    def remote(src, dst, send, recv, dev):
+        return pltpu.make_async_remote_copy(
+            src_ref=src, dst_ref=dst, send_sem=send, recv_sem=recv, device_id=dev, device_id_type=MESH
+        )
+
+    has_up = z < nz - 1
+    has_down = z > 0
+    barrier = pltpu.get_barrier_semaphore()
+    for d in range(4):
+        for other in range(2):
+            if d or other:
+                pl.semaphore_signal(barrier, inc=1, device_id=device(d, other), device_id_type=MESH)
+
+    @pl.when(has_up)
+    def _():
+        pl.semaphore_signal(barrier, inc=1, device_id=along(1), device_id_type=MESH)
+
+    @pl.when(has_down)
+    def _():
+        pl.semaphore_signal(barrier, inc=1, device_id=along(-1), device_id_type=MESH)
+
+    local_h = pltpu.make_async_copy(hidden_ref.at[:, quarter(0)], hbuf.at[0], ls.at[0])
+    local_w = pltpu.make_async_copy(w_ref.at[0, quarter(0)], wbuf.at[z, 0], ls.at[1])
+    slot = pl.ds(pl.multiple_of(a * rank, rank), rank)
+    local_e = [pltpu.make_async_copy(e_ref.at[0, j], ebuf.at[j, slot], ls.at[2 + j]) for j in range(2)]
+    local_h.start()
+    local_w.start()
+    for copy in local_e:
+        copy.start()
+    mbuf[0] = jnp.broadcast_to(idx_ref[...].astype(jnp.float32), (width, rows)).T.astype(jnp.bfloat16)
+    acc[...] = jnp.zeros_like(acc)
+    pl.semaphore_wait(barrier, 7 + has_up.astype(jnp.int32) + has_down.astype(jnp.int32))
+
+    def w_cross():
+        return remote(w_ref.at[0, quarter(2)], wbuf.at[z, 1], wxs, wxr, device(2))
+
+    def w_chain(way, zp, xr, own=False):
+        src = w_ref.at[0, quarter(0)] if own and xr == 0 else wbuf.at[zp, xr]
+        return remote(src, wbuf.at[zp, xr], wzs.at[way, zp, xr], wzr.at[zp, xr], along(1 - 2 * way))
+
+    def e_slot(zp):
+        return ebuf.at[y, pl.ds(pl.multiple_of((2 * zp + x) * rank, rank), rank)]
+
+    def e_chain(way, zp, own=False):
+        src = e_ref.at[0, y] if own else e_slot(zp)
+        return remote(src, e_slot(zp), ezs.at[way, zp], ezr.at[zp], along(1 - 2 * way))
+
+    def e_plane(d, zp, own=False):
+        src = e_ref.at[0, y] if own else e_slot(zp)
+        return remote(src, e_slot(zp), eps.at[zp, d], epr.at[zp, d], device(d))
+
+    def h_copy(d):
+        return remote(hidden_ref.at[:, quarter(d)], hbuf.at[d], hs.at[d], hr.at[d], device(d))
+
+    def m_copy(d):
+        return remote(mbuf.at[0], mbuf.at[d], ms.at[d], mr.at[d], device(d))
+
+    def p_copy(d, other):
+        return remote(pbuf.at[d], rbuf.at[d, other], ps.at[d, other], pr.at[d, other], device(d, other))
+
+    lanes = pl.ds(pl.multiple_of((1 - t) * feats, feats), feats)
+    base_copy = remote(base_ref.at[0, :, :, lanes], peer_base_ref, bs, br, device(0, 1))
+    ends = [has_up, has_down]
+
+    w_cross().start()
+    for way in range(2):
+        @pl.when(ends[way])
+        def _(way=way):
+            w_chain(way, z, 0, True).start()
+            e_chain(way, z, True).start()
+    for d in (1, 2, 3):
+        m_copy(d).start()
+        h_copy(d).start()
+    for d in (2, 3):
+        e_plane(d, z, True).start()
+    base_copy.start()
+
+    w_cross().wait_recv()
+    for way in range(2):
+        @pl.when(ends[way])
+        def _(way=way):
+            w_chain(way, z, 1).start()
+
+    def shrink(zp, xr):
+        number = (2 * zp + (1 - x if xr else x)).astype(jnp.float32)
+        part = jnp.dot(
+            hbuf[...].reshape(4 * rows, chunk), wbuf[zp, xr], preferred_element_type=jnp.float32
+        ).reshape(4, rows, width)
+        acc[...] = jnp.where(mbuf[...].astype(jnp.float32) == number, part, acc[...])
+
+    def held(way, k):
+        source = z - k if way == 0 else z + k
+        exists = z >= k if way == 0 else z + k < nz
+        return source, exists
+
+    for k in range(1, nz):
+        for xr in range(2):
+            for way in range(2):
+                source, exists = held(way, k)
+
+                @pl.when(exists)
+                def _(way=way, source=source, xr=xr, k=k):
+                    w_chain(way, source, xr).wait_recv()
+
+                @pl.when(jnp.logical_and(exists, ends[way]))
+                def _(way=way, source=source, xr=xr, k=k):
+                    w_chain(way, source, xr).start()
+
+                if xr == 0:
+                    @pl.when(exists)
+                    def _(way=way, source=source):
+                        e_chain(way, source).wait_recv()
+
+                    @pl.when(jnp.logical_and(exists, ends[way]))
+                    def _(way=way, source=source):
+                        e_chain(way, source).start()
+
+                    @pl.when(exists)
+                    def _(way=way, source=source):
+                        for d in (1, 2, 3):
+                            e_plane(d, source).start()
+                if k > 1:
+                    @pl.when(exists)
+                    def _(source=source, xr=xr):
+                        shrink(source, xr)
+        if k == 1:
+            local_h.wait()
+            local_w.wait()
+            for d in (1, 2, 3):
+                m_copy(d).wait_recv()
+                h_copy(d).wait_recv()
+            for xr in range(2):
+                shrink(z, xr)
+            for way in range(2):
+                source, exists = held(way, k)
+
+                @pl.when(exists)
+                def _(source=source):
+                    for xr in range(2):
+                        shrink(source, xr)
+
+    pbuf[...] = acc[...].astype(jnp.bfloat16)
+    for d in (3, 2, 1, 0):
+        for other in range(2):
+            if d or other:
+                p_copy(d, other).start()
+    for copy in local_e:
+        copy.wait()
+    for way in range(2):
+        for k in range(1, nz):
+            source, exists = held(way, k)
+
+            @pl.when(exists)
+            def _(source=source):
+                for d in (1, 2, 3):
+                    e_plane(d, source).wait_recv()
+    for d in (2, 3):
+        e_plane(d, z, True).wait_recv()
+    total = acc[0]
+    for d in range(4):
+        for other in range(2):
+            if d or other:
+                p_copy(d, other).wait_recv()
+                total = total + rbuf[d, other].astype(jnp.float32)
+    count = ebuf.shape[1] // rank
+    total = total.astype(jnp.bfloat16)
+    named = jnp.concatenate([mbuf[0].astype(jnp.float32)] * (count * rank // width), axis=1)
+    chosen = named == (lax.broadcasted_iota(jnp.int32, (rows, count * rank), 1) // rank).astype(jnp.float32)
+    for j in range(2):
+        one = jnp.concatenate([total[:, j * rank:(j + 1) * rank]] * count, axis=1)
+        spread = jnp.where(chosen, one.astype(jnp.float32), 0.0).astype(jnp.bfloat16)
+        delta_ref[:, j, :] = jnp.dot(spread, ebuf[j], preferred_element_type=jnp.float32)
+
+    base_copy.wait()
+    w_cross().wait_send()
+    for d in (1, 2, 3):
+        m_copy(d).wait_send()
+        h_copy(d).wait_send()
+    for d in (2, 3):
+        e_plane(d, z, True).wait_send()
+    for d in range(4):
+        for other in range(2):
+            if d or other:
+                p_copy(d, other).wait_send()
+    for way in range(2):
+        for k in range(nz):
+            source, exists = held(way, k)
+
+            @pl.when(jnp.logical_and(exists, ends[way]))
+            def _(way=way, source=source, k=k):
+                for xr in range(2):
+                    w_chain(way, source, xr, k == 0).wait_send()
+                e_chain(way, source, k == 0).wait_send()
+
+            if k:
+                @pl.when(exists)
+                def _(source=source):
+                    for d in (1, 2, 3):
+                        e_plane(d, source).wait_send()
+
+
+def local_planes(
+    hidden, row_adapter_index, adapter_shrink_weight, adapter_expand_weight, base_partial_sums
+):
+    nz = lax.axis_size("adapter") // 2
+    rows, width_here = hidden.shape
+    chunk = width_here // 4
+    width = adapter_shrink_weight.shape[2]
+    rank, feats = adapter_expand_weight.shape[2:]
+    dma = pltpu.SemaphoreType.DMA
+    hbm = pl.BlockSpec(memory_space=pl.ANY)
+    vmem = pl.BlockSpec(memory_space=pltpu.VMEM)
+    bf16 = jnp.bfloat16
+    delta, peer_base = pl.pallas_call(
+        functools.partial(plane_kernel, nz),
+        out_shape=(
+            jax.ShapeDtypeStruct((rows, 2, feats), jnp.float32),
+            jax.ShapeDtypeStruct((rows, 2, feats), bf16),
+        ),
+        in_specs=[hbm, vmem, hbm, hbm, hbm],
+        out_specs=(vmem, hbm),
+        scratch_shapes=[
+            pltpu.VMEM((4, rows, chunk), bf16),
+            pltpu.VMEM((4, rows, width), bf16),
+            pltpu.VMEM((nz, 2, chunk, width), bf16),
+            pltpu.VMEM((2, 2 * nz * rank, feats), bf16),
+            pltpu.VMEM((4, rows, width), jnp.float32),
+            pltpu.VMEM((4, rows, width), bf16),
+            pltpu.VMEM((4, 2, rows, width), bf16),
+            dma((4,)), dma((4,)), dma((4,)), dma((4,)),
+            dma, dma, dma((2, nz, 2)), dma((nz, 2)),
+            dma((2, nz)), dma((nz,)), dma((nz, 4)), dma((nz, 4)),
+            dma((4, 2)), dma((4, 2)), dma, dma, dma((4,)),
+        ],
+        compiler_params=pltpu.CompilerParams(
+            collective_id=0, has_side_effects=True, vmem_limit_bytes=60 * 1024 * 1024
+        ),
+    )(hidden, row_adapter_index.reshape(1, rows), adapter_shrink_weight, adapter_expand_weight, base_partial_sums)
+    own = lax.dynamic_slice_in_dim(base_partial_sums[0], lax.axis_index("tensor") * feats, feats, axis=2)
+    return (own.astype(jnp.float32) + peer_base.astype(jnp.float32) + delta).astype(bf16)
 
 
 def local(
@@ -65,4 +343,9 @@
         P("tensor", ("groups", "adapter"), None, None),
     )
     out_specs = P(("groups", "adapter"), None, "tensor")
-    return jax.shard_map(local, mesh=mesh, in_specs=in_specs, out_specs=out_specs, check_vma=False)
+    adapters = mesh.shape["adapter"]
+    planes = (
+        mesh.shape["groups"] == 2 and mesh.shape["tensor"] == 2 and adapters % 2 == 0 and 4 <= adapters <= 16
+    )
+    step = local_planes if planes else local
+    return jax.shard_map(step, mesh=mesh, in_specs=in_specs, out_specs=out_specs, check_vma=False)

time: 128 us -> 54 us (0.42)
  blocking collectives: 55.4 us -> 0 us
  Pallas kernels: 0 us -> 51.7 us
  waiting for transfers between devices: 42.7 us -> 0 us
  between operations: 13.5 us -> 0.02 us
  matrix products: 6.45 us -> 0 us
  starting transfers between devices: 5.8 us -> 0 us
  local copies, waits for them, and re-layouts: 2.82 us -> 0.01 us
  other arithmetic: 0.7 us -> 2.18 us
    all_to_all x1 -> x0, blocking collectives: 55.4 us -> none  [local(): lax.all_to_all(outgoing, 'adapter', split_axis=0, concat_axis=0, tiled=True)]
    pallas_call x0 -> x1, Pallas kernels: none -> 51.7 us  [local_planes(): pl.pallas_call(functools.partial(plane_kernel, nz), out_shape=(jax.ShapeD...]
    psum x1 -> x0, waiting for transfers between devices: 17.4 us -> none  [local(): lax.psum(jnp.einsum('ocw,wk->ock', lax.all_to_all(outgoing, 'adapter', sp...]
    all_to_all x1 -> x0, waiting for transfers between devices: 13.7 us -> none  [local(): lax.all_to_all(delta, 'adapter', split_axis=0, concat_axis=0, tiled=True)]
    reduce_scatter x1 -> x0, waiting for transfers between devices: 11.5 us -> none  [local(): lax.psum_scatter(base_partial_sums[0].astype(jnp.float32).astype(jnp.bflo...]
    dot_general x5 -> x0, matrix products: 6.45 us -> none  [the longest x1 2.48 us: local(): jnp.einsum('ocjk,jkf->ocjf', shrunk, expand_factor_table, precision=lax.P...]
    all_to_all x1 -> x0, starting transfers between devices: 5.76 us -> none  [local(): lax.all_to_all(delta, 'adapter', split_axis=0, concat_axis=0, tiled=True)]
    convert_element_type x3 -> x1, other arithmetic: 0.7 us -> 2.18 us  [local_planes(): (own.astype(jnp.float32) + peer_base.astype(jnp.float32) + delta).astype(...]
  transfers between devices with their start and end apart: 3 -> 0, of which waited for: 3 -> 0; matrix products, arithmetic and copies ran while one was open for 1% -> 0% of each run, Pallas kernels for 0% -> 0%
where the time goes in v1:
time: 54 us; the launch traced here: 53.9 us
  Pallas kernels  51.7 us (96%)
  other arithmetic  2.18 us (4%)
    pallas_call x1, Pallas kernels, local_planes(): pl.pallas_call(functools.partial(plane_kernel, nz), out_shape=(jax.ShapeD...  51.7 us
    convert_element_type x1, other arithmetic, local_planes(): (own.astype(jnp.float32) + peer_base.astype(jnp.float32) + delta).astype(...  2.18 us

profile of v1, /device:TPU:0, one launch (start us, length us, event | category | flops | bytes accessed | tf_op | source)
XLA Modules:
  0.0 53.9 jit_solution(7910397809375050456)
XLA Ops:
  0.0 0.0 copy-start
  0.0 51.7 %shard_map.55 = (f32[128,2,512]{2,1,0:T(2,128)}, bf16[128,2,512]{2,1,0:T(2,128)(2,1)}) custom-call(bf16[128,4096]{1,0:T(8,128)(2,1)} %hidden_ref.1, s32[1,128]{1,0:T(1,128)} %bitcast.4, bf16[1,4096,128]{2,1,0:T(8,128)(2,1)} %w_ref.1, bf16[1,2,64,512]{3,2,1,0:T(8,128)(2,1)} %e_ref.1, bf16[1,128,2,1024]{3,2,1,0:T(2,128)(2,1)} %base_ref.1), custom_call_target="tpu_custom_call" | custom-call | tf_op jit(solution)/shard_map/pallas_call | solution.py:256
  51.7 0.0 copy-done
  51.7 2.2 %fusion.1 = bf16[128,2,512]{2,1,0:T(2,128)(2,1)} fusion(f32[128,2,512]{2,1,0:T(2,128)} %get-tuple-element.8, bf16[128,2,512]{2,1,0:T(2,128)(2,1)} %get-tuple-element.7, bf16[1,128,2,1024]{3,2,1,0:T(2,128)(2,1)S(1)} %copy-done, s32[]{:T(128)S(6)} %select_n.3), kind=kLoop, calls=%fused_computation.2 | loop fusion | flops 655360 | bytes 1310724 | tf_op jit(solution)/shard_map/convert_element_type | solution.py:282
Async XLA Ops:
  0.0 51.7 %copy-start = (bf16[1,128,2,1024]{3,2,1,0:T(2,128)(2,1)S(1)}, bf16[1,128,2,1024]{3,2,1,0:T(2,128)(2,1)}, u32[]{:S(2)}) copy-start(bf16[1,128,2,1024]{3,2,1,0:T(2,128)(2,1)} %base_ref.1) | copy-start | bytes 1572868

commit v2 on v1

--- a/solution.py
+++ b/solution.py
@@ -8,12 +8,13 @@
 from jax.sharding import PartitionSpec as P
 
 MESH = pl.DeviceIdType.MESH
+HI_EIGHTHS = 3
 
 
 def plane_kernel(
     nz, hidden_ref, idx_ref, w_ref, e_ref, base_ref, delta_ref, peer_base_ref,
-    hbuf, mbuf, wbuf, ebuf, acc, pbuf, rbuf,
-    hs, hr, ms, mr, wxs, wxr, wzs, wzr, ezs, ezr, eps, epr, ps, pr, bs, br, ls,
+    hbuf, mbuf, wbuf, ebuf, acc, pbuf, rbuf, hbuf2, mbuf2, acc2, pbuf2, abuf,
+    hs, hr, ms, mr, wxs, wxr, wzs, wzr, ezs, ezr, eps, epr, ps, pr, bs, br, ls, xs, xr_, as_, ar,
 ):
     y = lax.axis_index("groups")
     a = lax.axis_index("adapter")
@@ -25,6 +26,12 @@
     rank = e_ref.shape[2]
     feats = e_ref.shape[3]
     width = w_ref.shape[2]
+    hi = hbuf2.shape[2]
+    lo = chunk - hi
+    last = nz - 1
+    is_end = z % last == 0
+    is_inner = z % last != 0
+    by_end = jnp.logical_and(is_inner, (z - 1) % (last - 2) == 0)
 
     def coords(d):
         return (1 - x if d // 2 else x), (1 - y if d % 2 else y)
@@ -76,9 +83,52 @@
     def w_cross():
         return remote(w_ref.at[0, quarter(2)], wbuf.at[z, 1], wxs, wxr, device(2))
 
-    def w_chain(way, zp, xr, own=False):
-        src = w_ref.at[0, quarter(0)] if own and xr == 0 else wbuf.at[zp, xr]
-        return remote(src, wbuf.at[zp, xr], wzs.at[way, zp, xr], wzr.at[zp, xr], along(1 - 2 * way))
+    def w_chain(way, zp, xr, size, own=False):
+        here = wbuf.at[zp, xr, pl.ds(0, size)]
+        src = w_ref.at[0, pl.ds(pl.multiple_of((2 * x + y) * chunk, chunk), size)] if own and xr == 0 else here
+        return remote(src, here, wzs.at[way, zp, xr], wzr.at[zp, xr], along(1 - 2 * way))
+
+    to_end = [z + 1 == last, z == 1]
+    to_inner = [z + 1 != last, z != 1]
+
+    def w_send(way, zp, xr, own=False):
+        @pl.when(to_end[way])
+        def _():
+            w_chain(way, zp, xr, lo, own).start()
+
+        @pl.when(to_inner[way])
+        def _():
+            w_chain(way, zp, xr, chunk, own).start()
+
+    def w_sent(way, zp, xr, own=False):
+        @pl.when(to_end[way])
+        def _():
+            w_chain(way, zp, xr, lo, own).wait_send()
+
+        @pl.when(to_inner[way])
+        def _():
+            w_chain(way, zp, xr, chunk, own).wait_send()
+
+    def w_arrived(way, zp, xr):
+        @pl.when(is_end)
+        def _():
+            w_chain(way, zp, xr, lo).wait_recv()
+
+        @pl.when(is_inner)
+        def _():
+            w_chain(way, zp, xr, chunk).wait_recv()
+
+    inward = 1 - 2 * (z // last)
+    outward = 2 * (z // (last - 1)) - 1
+
+    def hi_copy(d):
+        return remote(hbuf.at[d, :, pl.ds(lo, hi)], hbuf2.at[d], xs.at[d], xr_.at[d], along(inward))
+
+    def m2_copy():
+        return remote(mbuf, mbuf2, xs.at[4], xr_.at[4], along(inward))
+
+    def a_copy():
+        return remote(pbuf2, abuf, as_, ar, along(outward))
 
     def e_slot(zp):
         return ebuf.at[y, pl.ds(pl.multiple_of((2 * zp + x) * rank, rank), rank)]
@@ -108,8 +158,7 @@
     for way in range(2):
         @pl.when(ends[way])
         def _(way=way):
-            w_chain(way, z, 0, True).start()
-            e_chain(way, z, True).start()
+            w_send(way, z, 0, True)
     for d in (1, 2, 3):
         m_copy(d).start()
         h_copy(d).start()
@@ -121,14 +170,38 @@
     for way in range(2):
         @pl.when(ends[way])
         def _(way=way):
-            w_chain(way, z, 1).start()
+            w_send(way, z, 1)
+            e_chain(way, z, True).start()
+
+    local_h.wait()
+    local_w.wait()
+
+    @pl.when(is_end)
+    def _():
+        for d in (1, 2, 3):
+            m_copy(d).wait_recv()
+            h_copy(d).wait_recv()
+        m2_copy().start()
+        for d in range(4):
+            hi_copy(d).start()
 
     def shrink(zp, xr):
         number = (2 * zp + (1 - x if xr else x)).astype(jnp.float32)
-        part = jnp.dot(
-            hbuf[...].reshape(4 * rows, chunk), wbuf[zp, xr], preferred_element_type=jnp.float32
-        ).reshape(4, rows, width)
-        acc[...] = jnp.where(mbuf[...].astype(jnp.float32) == number, part, acc[...])
+        names = mbuf[...].astype(jnp.float32) == number
+
+        @pl.when(is_end)
+        def _():
+            part = jnp.dot(
+                hbuf[:, :, :lo].reshape(4 * rows, lo), wbuf[zp, xr, :lo], preferred_element_type=jnp.float32
+            ).reshape(4, rows, width)
+            acc[...] = jnp.where(names, part, acc[...])
+
+        @pl.when(is_inner)
+        def _():
+            part = jnp.dot(
+                hbuf[...].reshape(4 * rows, chunk), wbuf[zp, xr], preferred_element_type=jnp.float32
+            ).reshape(4, rows, width)
+            acc[...] = jnp.where(names, part, acc[...])
 
     def held(way, k):
         source = z - k if way == 0 else z + k
@@ -142,13 +215,13 @@
 
                 @pl.when(exists)
                 def _(way=way, source=source, xr=xr, k=k):
-                    w_chain(way, source, xr).wait_recv()
+                    w_arrived(way, source, xr)
 
                 @pl.when(jnp.logical_and(exists, ends[way]))
                 def _(way=way, source=source, xr=xr, k=k):
-                    w_chain(way, source, xr).start()
-
-                if xr == 0:
+                    w_send(way, source, xr)
+
+                if xr == 1:
                     @pl.when(exists)
                     def _(way=way, source=source):
                         e_chain(way, source).wait_recv()
@@ -166,11 +239,11 @@
                     def _(source=source, xr=xr):
                         shrink(source, xr)
         if k == 1:
-            local_h.wait()
-            local_w.wait()
-            for d in (1, 2, 3):
-                m_copy(d).wait_recv()
-                h_copy(d).wait_recv()
+            @pl.when(is_inner)
+            def _():
+                for d in (1, 2, 3):
+                    m_copy(d).wait_recv()
+                    h_copy(d).wait_recv()
             for xr in range(2):
                 shrink(z, xr)
             for way in range(2):
@@ -180,12 +253,38 @@
                 def _(source=source):
                     for xr in range(2):
                         shrink(source, xr)
+
+    @pl.when(is_end)
+    def _():
+        a_copy().wait_recv()
+        acc[...] += abuf[...].astype(jnp.float32)
 
     pbuf[...] = acc[...].astype(jnp.bfloat16)
     for d in (3, 2, 1, 0):
         for other in range(2):
             if d or other:
                 p_copy(d, other).start()
+
+    @pl.when(by_end)
+    def _():
+        m2_copy().wait_recv()
+        for d in range(4):
+            hi_copy(d).wait_recv()
+        acc2[...] = jnp.zeros_like(acc2)
+
+        def one(i, carry):
+            zp, xr = i // 2, i % 2
+            number = (2 * zp + (x + xr) % 2).astype(jnp.float32)
+            part = jnp.dot(
+                hbuf2[...].reshape(4 * rows, hi), wbuf[zp, xr, lo:], preferred_element_type=jnp.float32
+            ).reshape(4, rows, width)
+            acc2[...] = jnp.where(mbuf2[...].astype(jnp.float32) == number, part, acc2[...])
+            return carry
+
+        lax.fori_loop(0, 2 * nz, one, 0)
+        pbuf2[...] = acc2[...].astype(jnp.bfloat16)
+        a_copy().start()
+
     for copy in local_e:
         copy.wait()
     for way in range(2):
@@ -213,6 +312,16 @@
         spread = jnp.where(chosen, one.astype(jnp.float32), 0.0).astype(jnp.bfloat16)
         delta_ref[:, j, :] = jnp.dot(spread, ebuf[j], preferred_element_type=jnp.float32)
 
+    @pl.when(is_end)
+    def _():
+        m2_copy().wait_send()
+        for d in range(4):
+            hi_copy(d).wait_send()
+
+    @pl.when(by_end)
+    def _():
+        a_copy().wait_send()
+
     base_copy.wait()
     w_cross().wait_send()
     for d in (1, 2, 3):
@@ -231,7 +340,7 @@
             @pl.when(jnp.logical_and(exists, ends[way]))
             def _(way=way, source=source, k=k):
                 for xr in range(2):
-                    w_chain(way, source, xr, k == 0).wait_send()
+                    w_sent(way, source, xr, k == 0)
                 e_chain(way, source, k == 0).wait_send()
 
             if k:
@@ -247,6 +356,7 @@
     nz = lax.axis_size("adapter") // 2
     rows, width_here = hidden.shape
     chunk = width_here // 4
+    hi = chunk * HI_EIGHTHS // 8
     width = adapter_shrink_weight.shape[2]
     rank, feats = adapter_expand_weight.shape[2:]
     dma = pltpu.SemaphoreType.DMA
@@ -269,10 +379,16 @@
             pltpu.VMEM((4, rows, width), jnp.float32),
             pltpu.VMEM((4, rows, width), bf16),
             pltpu.VMEM((4, 2, rows, width), bf16),
+            pltpu.VMEM((4, rows, hi), bf16),
+            pltpu.VMEM((4, rows, width), bf16),
+            pltpu.VMEM((4, rows, width), jnp.float32),
+            pltpu.VMEM((4, rows, width), bf16),
+            pltpu.VMEM((4, rows, width), bf16),
             dma((4,)), dma((4,)), dma((4,)), dma((4,)),
             dma, dma, dma((2, nz, 2)), dma((nz, 2)),
             dma((2, nz)), dma((nz,)), dma((nz, 4)), dma((nz, 4)),
             dma((4, 2)), dma((4, 2)), dma, dma, dma((4,)),
+            dma((5,)), dma((5,)), dma, dma,
         ],
         compiler_params=pltpu.CompilerParams(
             collective_id=0, has_side_effects=True, vmem_limit_bytes=60 * 1024 * 1024
@@ -345,7 +461,7 @@
     out_specs = P(("groups", "adapter"), None, "tensor")
     adapters = mesh.shape["adapter"]
     planes = (
-        mesh.shape["groups"] == 2 and mesh.shape["tensor"] == 2 and adapters % 2 == 0 and 4 <= adapters <= 16
+        mesh.shape["groups"] == 2 and mesh.shape["tensor"] == 2 and adapters % 2 == 0 and 8 <= adapters <= 16
     )
     step = local_planes if planes else local
     return jax.shard_map(step, mesh=mesh, in_specs=in_specs, out_specs=out_specs, check_vma=False)

time: 54 us -> 52.5 us (0.972)
  Pallas kernels: 51.7 us -> 50.2 us
    pallas_call x1, Pallas kernels: 51.7 us -> 50.2 us  [local_planes(): pl.pallas_call(functools.partial(plane_kernel, nz), out_shape=(jax.ShapeD...]
where the time goes in v2:
time: 52.5 us; the launch traced here: 52.4 us
  Pallas kernels  50.2 us (96%)
  other arithmetic  2.18 us (4%)
    pallas_call x1, Pallas kernels, local_planes(): pl.pallas_call(functools.partial(plane_kernel, nz), out_shape=(jax.ShapeD...  50.2 us
    convert_element_type x1, other arithmetic, local_planes(): (own.astype(jnp.float32) + peer_base.astype(jnp.float32) + delta).astype(...  2.18 us

profile of v2, /device:TPU:0, one launch (start us, length us, event | category | flops | bytes accessed | tf_op | source)
XLA Modules:
  0.0 52.4 jit_solution(9702024053970109242)
XLA Ops:
  0.0 0.0 copy-start
  0.0 50.2 %shard_map.55 = (f32[128,2,512]{2,1,0:T(2,128)}, bf16[128,2,512]{2,1,0:T(2,128)(2,1)}) custom-call(bf16[128,4096]{1,0:T(8,128)(2,1)} %hidden_ref.1, s32[1,128]{1,0:T(1,128)} %bitcast.4, bf16[1,4096,128]{2,1,0:T(8,128)(2,1)} %w_ref.1, bf16[1,2,64,512]{3,2,1,0:T(8,128)(2,1)} %e_ref.1, bf16[1,128,2,1024]{3,2,1,0:T(2,128)(2,1)} %base_ref.1), custom_call_target="tpu_custom_call" | custom-call | tf_op jit(solution)/shard_map/pallas_call | solution.py:366
  50.2 0.0 copy-done
  50.2 2.2 %fusion.1 = bf16[128,2,512]{2,1,0:T(2,128)(2,1)} fusion(f32[128,2,512]{2,1,0:T(2,128)} %get-tuple-element.8, bf16[128,2,512]{2,1,0:T(2,128)(2,1)} %get-tuple-element.7, bf16[1,128,2,1024]{3,2,1,0:T(2,128)(2,1)S(1)} %copy-done, s32[]{:T(128)S(6)} %select_n.3), kind=kLoop, calls=%fused_computation.2 | loop fusion | flops 655360 | bytes 1310724 | tf_op jit(solution)/shard_map/convert_element_type | solution.py:398
Async XLA Ops:
  0.0 50.2 %copy-start = (bf16[1,128,2,1024]{3,2,1,0:T(2,128)(2,1)S(1)}, bf16[1,128,2,1024]{3,2,1,0:T(2,128)(2,1)}, u32[]{:S(2)}) copy-start(bf16[1,128,2,1024]{3,2,1,0:T(2,128)(2,1)} %base_ref.1) | copy-start | bytes 1572868

commit v3 on v1

--- a/solution.py
+++ b/solution.py
@@ -8,12 +8,13 @@
 from jax.sharding import PartitionSpec as P
 
 MESH = pl.DeviceIdType.MESH
+HI_EIGHTHS = 3
 
 
 def plane_kernel(
     nz, hidden_ref, idx_ref, w_ref, e_ref, base_ref, delta_ref, peer_base_ref,
-    hbuf, mbuf, wbuf, ebuf, acc, pbuf, rbuf,
-    hs, hr, ms, mr, wxs, wxr, wzs, wzr, ezs, ezr, eps, epr, ps, pr, bs, br, ls,
+    hbuf, mbuf, wbuf, ebuf, acc, pbuf, rbuf, hbuf2, mbuf2, acc2, pbuf2, abuf,
+    hs, hr, ms, mr, wxs, wxr, wzs, wzr, ezs, ezr, eps, epr, ps, pr, bs, br, ls, xs, xr_, as_, ar,
 ):
     y = lax.axis_index("groups")
     a = lax.axis_index("adapter")
@@ -25,6 +26,13 @@
     rank = e_ref.shape[2]
     feats = e_ref.shape[3]
     width = w_ref.shape[2]
+    hi = hbuf2.shape[2]
+    lo = chunk - hi
+    last = nz - 1
+    is_end = z % last == 0
+    is_inner = z % last != 0
+    inward = 1 - 2 * (z // last)
+    outward = 2 * (z // (last - 1)) - 1
 
     def coords(d):
         return (1 - x if d // 2 else x), (1 - y if d % 2 else y)
@@ -76,16 +84,38 @@
     def w_cross():
         return remote(w_ref.at[0, quarter(2)], wbuf.at[z, 1], wxs, wxr, device(2))
 
-    def w_chain(way, zp, xr, own=False):
-        src = w_ref.at[0, quarter(0)] if own and xr == 0 else wbuf.at[zp, xr]
-        return remote(src, wbuf.at[zp, xr], wzs.at[way, zp, xr], wzr.at[zp, xr], along(1 - 2 * way))
+    def w_copy(step, way, zp, xr, size, own=False):
+        here = wbuf.at[zp, xr, pl.ds(0, size)]
+        src = w_ref.at[0, pl.ds(pl.multiple_of((2 * x + y) * chunk, chunk), size)] if own else here
+        return remote(src, here, wzs.at[way, zp, xr], wzr.at[zp, xr], along(step))
+
+    def w_out(zp, xr, own=False):
+        return w_copy(outward, 0, zp, xr, lo, own)
+
+    def w_across(zp, xr, own=False):
+        return w_copy(-outward, 1, zp, xr, chunk, own)
+
+    def w_in(zp, xr, own=False):
+        return w_copy(inward, 0, zp, xr, chunk, own)
+
+    def w_got(zp, xr):
+        return w_copy(inward, 0, zp, xr, lo)
+
+    def hi_copy(d):
+        return remote(hbuf.at[d, :, pl.ds(lo, hi)], hbuf2.at[d], xs.at[d], xr_.at[d], along(inward))
+
+    def m2_copy():
+        return remote(mbuf, mbuf2, xs.at[4], xr_.at[4], along(inward))
+
+    def a_copy():
+        return remote(pbuf2, abuf, as_, ar, along(outward))
 
     def e_slot(zp):
         return ebuf.at[y, pl.ds(pl.multiple_of((2 * zp + x) * rank, rank), rank)]
 
-    def e_chain(way, zp, own=False):
+    def e_chain(step, way, zp, own=False):
         src = e_ref.at[0, y] if own else e_slot(zp)
-        return remote(src, e_slot(zp), ezs.at[way, zp], ezr.at[zp], along(1 - 2 * way))
+        return remote(src, e_slot(zp), ezs.at[way, zp], ezr.at[zp], along(step))
 
     def e_plane(d, zp, own=False):
         src = e_ref.at[0, y] if own else e_slot(zp)
@@ -102,100 +132,151 @@
 
     lanes = pl.ds(pl.multiple_of((1 - t) * feats, feats), feats)
     base_copy = remote(base_ref.at[0, :, :, lanes], peer_base_ref, bs, br, device(0, 1))
-    ends = [has_up, has_down]
 
     w_cross().start()
-    for way in range(2):
-        @pl.when(ends[way])
-        def _(way=way):
-            w_chain(way, z, 0, True).start()
-            e_chain(way, z, True).start()
     for d in (1, 2, 3):
         m_copy(d).start()
+    h_copy(1).start()
+
+    @pl.when(is_inner)
+    def _():
+        w_out(z, 0, True).start()
+        w_across(z, 0, True).start()
+
+    @pl.when(is_end)
+    def _():
+        w_in(z, 0, True).start()
+
+    base_copy.start()
+    local_h.wait()
+    local_w.wait()
+    w_cross().wait_recv()
+    for d in (2, 3):
         h_copy(d).start()
-    for d in (2, 3):
-        e_plane(d, z, True).start()
-    base_copy.start()
-
-    w_cross().wait_recv()
-    for way in range(2):
-        @pl.when(ends[way])
-        def _(way=way):
-            w_chain(way, z, 1).start()
-
-    def shrink(zp, xr):
+
+    def spread(zp):
+        e_chain(inward, 0, zp).wait_recv()
+        for d in (1, 2, 3):
+            e_plane(d, zp).start()
+
+    def send_partials():
+        pbuf[...] = acc[...].astype(jnp.bfloat16)
+        for d in (3, 2, 1, 0):
+            for other in range(2):
+                if d or other:
+                    p_copy(d, other).start()
+
+    def shrink(zp, xr, size):
         number = (2 * zp + (1 - x if xr else x)).astype(jnp.float32)
         part = jnp.dot(
-            hbuf[...].reshape(4 * rows, chunk), wbuf[zp, xr], preferred_element_type=jnp.float32
+            hbuf[:, :, :size].reshape(4 * rows, size), wbuf[zp, xr, :size], preferred_element_type=jnp.float32
         ).reshape(4, rows, width)
         acc[...] = jnp.where(mbuf[...].astype(jnp.float32) == number, part, acc[...])
 
-    def held(way, k):
-        source = z - k if way == 0 else z + k
-        exists = z >= k if way == 0 else z + k < nz
-        return source, exists
-
-    for k in range(1, nz):
+    def shrink_end(zp, xr):
+        number = (2 * zp + (x + xr) % 2).astype(jnp.float32)
+        part = jnp.dot(
+            hbuf2[...].reshape(4 * rows, hi), wbuf[zp, xr, lo:], preferred_element_type=jnp.float32
+        ).reshape(4, rows, width)
+        acc2[...] = jnp.where(mbuf2[...].astype(jnp.float32) == number, part, acc2[...])
+
+    @pl.when(is_inner)
+    def _():
+        zn, zo = z + outward, last - z
+        zf = last - zn
+        w_out(z, 0, True).wait_send()
+        w_out(z, 1).start()
+        w_across(zn, 0).wait_recv()
+        w_across(z, 0, True).wait_send()
+        w_across(zn, 0).start()
+        w_across(zo, 0).wait_recv()
+        w_out(z, 1).wait_send()
+        e_chain(outward, 0, z, True).start()
+        w_out(zo, 0).start()
+        w_across(zn, 1).wait_recv()
+        w_across(zn, 0).wait_send()
+        w_across(zn, 1).start()
+        for d in (2, 3):
+            e_plane(d, z, True).start()
+        acc2[...] = jnp.zeros_like(acc2)
+        w_across(zf, 0).wait_recv()
+        w_out(zo, 0).wait_send()
+        w_out(zf, 0).start()
+        spread(zn)
+        w_across(zn, 1).wait_send()
+        e_chain(-outward, 1, zn).start()
+        w_across(z, 1).start()
+        for d in (1, 2, 3):
+            m_copy(d).wait_recv()
+            h_copy(d).wait_recv()
+        for zp, xr in ((z, 0), (z, 1), (zn, 0), (zn, 1), (zo, 0), (zf, 0)):
+            shrink(zp, xr, chunk)
+        w_across(zf, 1).wait_recv()
+        w_out(zf, 0).wait_send()
+        w_out(zf, 1).start()
+        shrink(zf, 1, chunk)
+        m2_copy().wait_recv()
+        for d in range(4):
+            hi_copy(d).wait_recv()
+
+        lax.fori_loop(0, nz, lambda i, c: (shrink_end(i, 0), c)[1], 0)
+        lax.fori_loop(1, nz, lambda i, c: (shrink_end((zo + i) % nz, 1), c)[1], 0)
+        spread(zf)
+        e_chain(outward, 0, zf).start()
+        w_across(z, 1).wait_send()
+        e_chain(-outward, 1, z, True).start()
+        w_across(zo, 1).wait_recv()
+        w_out(zf, 1).wait_send()
+        w_out(zo, 1).start()
+        shrink_end(zo, 1)
+        pbuf2[...] = acc2[...].astype(jnp.bfloat16)
+        a_copy().start()
+        shrink(zo, 1, chunk)
+        send_partials()
+        spread(zo)
+        e_chain(outward, 0, zo).start()
+
+    @pl.when(is_end)
+    def _():
+        zi, zf = z + inward, last - z
+        zo = last - zi
+        w_in(z, 0, True).wait_send()
+        w_in(z, 1).start()
+        w_in(z, 1).wait_send()
+        e_chain(inward, 0, z, True).start()
+        hi_copy(0).start()
+        h_copy(1).wait_recv()
+        hi_copy(1).start()
+        for d in (2, 3):
+            e_plane(d, z, True).start()
+        for d in (1, 2, 3):
+            m_copy(d).wait_recv()
+        m2_copy().start()
+        for d in (2, 3):
+            h_copy(d).wait_recv()
+            hi_copy(d).start()
+        shrink(z, 0, lo)
+        shrink(z, 1, lo)
         for xr in range(2):
-            for way in range(2):
-                source, exists = held(way, k)
-
-                @pl.when(exists)
-                def _(way=way, source=source, xr=xr, k=k):
-                    w_chain(way, source, xr).wait_recv()
-
-                @pl.when(jnp.logical_and(exists, ends[way]))
-                def _(way=way, source=source, xr=xr, k=k):
-                    w_chain(way, source, xr).start()
-
-                if xr == 0:
-                    @pl.when(exists)
-                    def _(way=way, source=source):
-                        e_chain(way, source).wait_recv()
-
-                    @pl.when(jnp.logical_and(exists, ends[way]))
-                    def _(way=way, source=source):
-                        e_chain(way, source).start()
-
-                    @pl.when(exists)
-                    def _(way=way, source=source):
-                        for d in (1, 2, 3):
-                            e_plane(d, source).start()
-                if k > 1:
-                    @pl.when(exists)
-                    def _(source=source, xr=xr):
-                        shrink(source, xr)
-        if k == 1:
-            local_h.wait()
-            local_w.wait()
-            for d in (1, 2, 3):
-                m_copy(d).wait_recv()
-                h_copy(d).wait_recv()
-            for xr in range(2):
-                shrink(z, xr)
-            for way in range(2):
-                source, exists = held(way, k)
-
-                @pl.when(exists)
-                def _(source=source):
-                    for xr in range(2):
-                        shrink(source, xr)
-
-    pbuf[...] = acc[...].astype(jnp.bfloat16)
-    for d in (3, 2, 1, 0):
-        for other in range(2):
-            if d or other:
-                p_copy(d, other).start()
+            w_got(zi, xr).wait_recv()
+            shrink(zi, xr, lo)
+        spread(zi)
+        for zp, xr in ((zo, 0), (zf, 0), (zf, 1)):
+            w_got(zp, xr).wait_recv()
+            shrink(zp, xr, lo)
+        spread(zf)
+        w_got(zo, 1).wait_recv()
+        shrink(zo, 1, lo)
+        a_copy().wait_recv()
+        acc[...] += abuf[...].astype(jnp.float32)
+        send_partials()
+        spread(zo)
+
     for copy in local_e:
         copy.wait()
-    for way in range(2):
-        for k in range(1, nz):
-            source, exists = held(way, k)
-
-            @pl.when(exists)
-            def _(source=source):
-                for d in (1, 2, 3):
-                    e_plane(d, source).wait_recv()
+    for k in range(1, nz):
+        for d in (1, 2, 3):
+            e_plane(d, (z + k) % nz).wait_recv()
     for d in (2, 3):
         e_plane(d, z, True).wait_recv()
     total = acc[0]
@@ -213,6 +294,25 @@
         spread = jnp.where(chosen, one.astype(jnp.float32), 0.0).astype(jnp.bfloat16)
         delta_ref[:, j, :] = jnp.dot(spread, ebuf[j], preferred_element_type=jnp.float32)
 
+    @pl.when(is_end)
+    def _():
+        m2_copy().wait_send()
+        for d in range(4):
+            hi_copy(d).wait_send()
+        e_chain(inward, 0, z, True).wait_send()
+
+    @pl.when(is_inner)
+    def _():
+        zn, zo = z + outward, last - z
+        zf = last - zn
+        a_copy().wait_send()
+        w_out(zo, 1).wait_send()
+        for zp in (zo, zf):
+            e_chain(outward, 0, zp).wait_send()
+        e_chain(outward, 0, z, True).wait_send()
+        e_chain(-outward, 1, zn).wait_send()
+        e_chain(-outward, 1, z, True).wait_send()
+
     base_copy.wait()
     w_cross().wait_send()
     for d in (1, 2, 3):
@@ -224,21 +324,9 @@
         for other in range(2):
             if d or other:
                 p_copy(d, other).wait_send()
-    for way in range(2):
-        for k in range(nz):
-            source, exists = held(way, k)
-
-            @pl.when(jnp.logical_and(exists, ends[way]))
-            def _(way=way, source=source, k=k):
-                for xr in range(2):
-                    w_chain(way, source, xr, k == 0).wait_send()
-                e_chain(way, source, k == 0).wait_send()
-
-            if k:
-                @pl.when(exists)
-                def _(source=source):
-                    for d in (1, 2, 3):
-                        e_plane(d, source).wait_send()
+    for k in range(1, nz):
+        for d in (1, 2, 3):
+            e_plane(d, (z + k) % nz).wait_send()
 
 
 def local_planes(
@@ -247,6 +335,7 @@
     nz = lax.axis_size("adapter") // 2
     rows, width_here = hidden.shape
     chunk = width_here // 4
+    hi = chunk * HI_EIGHTHS // 8
     width = adapter_shrink_weight.shape[2]
     rank, feats = adapter_expand_weight.shape[2:]
     dma = pltpu.SemaphoreType.DMA
@@ -269,10 +358,16 @@
             pltpu.VMEM((4, rows, width), jnp.float32),
             pltpu.VMEM((4, rows, width), bf16),
             pltpu.VMEM((4, 2, rows, width), bf16),
+            pltpu.VMEM((4, rows, hi), bf16),
+            pltpu.VMEM((4, rows, width), bf16),
+            pltpu.VMEM((4, rows, width), jnp.float32),
+            pltpu.VMEM((4, rows, width), bf16),
+            pltpu.VMEM((4, rows, width), bf16),
             dma((4,)), dma((4,)), dma((4,)), dma((4,)),
             dma, dma, dma((2, nz, 2)), dma((nz, 2)),
             dma((2, nz)), dma((nz,)), dma((nz, 4)), dma((nz, 4)),
             dma((4, 2)), dma((4, 2)), dma, dma, dma((4,)),
+            dma((5,)), dma((5,)), dma, dma,
         ],
         compiler_params=pltpu.CompilerParams(
             collective_id=0, has_side_effects=True, vmem_limit_bytes=60 * 1024 * 1024
@@ -345,7 +440,7 @@
     out_specs = P(("groups", "adapter"), None, "tensor")
     adapters = mesh.shape["adapter"]
     planes = (
-        mesh.shape["groups"] == 2 and mesh.shape["tensor"] == 2 and adapters % 2 == 0 and 4 <= adapters <= 16
+        mesh.shape["groups"] == 2 and mesh.shape["tensor"] == 2 and adapters == 8
     )
     step = local_planes if planes else local
     return jax.shard_map(step, mesh=mesh, in_specs=in_specs, out_specs=out_specs, check_vma=False)

time: 54 us -> 53 us (0.981)
  Pallas kernels: 51.7 us -> 50.6 us
    pallas_call x1, Pallas kernels: 51.7 us -> 50.6 us  [local_planes(): pl.pallas_call(functools.partial(plane_kernel, nz), out_shape=(jax.ShapeD...]
where the time goes in v3:
time: 53 us; the launch traced here: 52.8 us
  Pallas kernels  50.6 us (95%)
  other arithmetic  2.18 us (4%)
    pallas_call x1, Pallas kernels, local_planes(): pl.pallas_call(functools.partial(plane_kernel, nz), out_shape=(jax.ShapeD...  50.6 us
    convert_element_type x1, other arithmetic, local_planes(): (own.astype(jnp.float32) + peer_base.astype(jnp.float32) + delta).astype(...  2.18 us

profile of v3, /device:TPU:0, one launch (start us, length us, event | category | flops | bytes accessed | tf_op | source)
XLA Modules:
  0.0 52.8 jit_solution(9325297151580233790)
XLA Ops:
  0.0 0.0 copy-start
  0.0 50.6 %shard_map.55 = (f32[128,2,512]{2,1,0:T(2,128)}, bf16[128,2,512]{2,1,0:T(2,128)(2,1)}) custom-call(bf16[128,4096]{1,0:T(8,128)(2,1)} %hidden_ref.1, s32[1,128]{1,0:T(1,128)} %bitcast.4, bf16[1,4096,128]{2,1,0:T(8,128)(2,1)} %w_ref.1, bf16[1,2,64,512]{3,2,1,0:T(8,128)(2,1)} %e_ref.1, bf16[1,128,2,1024]{3,2,1,0:T(2,128)(2,1)} %base_ref.1), custom_call_target="tpu_custom_call" | custom-call | tf_op jit(solution)/shard_map/pallas_call | solution.py:345
  50.6 0.0 copy-done
  50.6 2.2 %fusion.1 = bf16[128,2,512]{2,1,0:T(2,128)(2,1)} fusion(f32[128,2,512]{2,1,0:T(2,128)} %get-tuple-element.8, bf16[128,2,512]{2,1,0:T(2,128)(2,1)} %get-tuple-element.7, bf16[1,128,2,1024]{3,2,1,0:T(2,128)(2,1)S(1)} %copy-done, s32[]{:T(128)S(6)} %select_n.3), kind=kLoop, calls=%fused_computation.2 | loop fusion | flops 655360 | bytes 1310724 | tf_op jit(solution)/shard_map/convert_element_type | solution.py:377
Async XLA Ops:
  0.0 50.6 %copy-start = (bf16[1,128,2,1024]{3,2,1,0:T(2,128)(2,1)S(1)}, bf16[1,128,2,1024]{3,2,1,0:T(2,128)(2,1)}, u32[]{:S(2)}) copy-start(bf16[1,128,2,1024]{3,2,1,0:T(2,128)(2,1)} %base_ref.1) | copy-start | bytes 1572868

commit v4 on v3

--- a/solution.py
+++ b/solution.py
@@ -184,27 +184,26 @@
     def _():
         zn, zo = z + outward, last - z
         zf = last - zn
-        w_out(z, 0, True).wait_send()
         w_out(z, 1).start()
         w_across(zn, 0).wait_recv()
-        w_across(z, 0, True).wait_send()
         w_across(zn, 0).start()
         w_across(zo, 0).wait_recv()
-        w_out(z, 1).wait_send()
+        w_out(z, 0, True).wait_send()
         e_chain(outward, 0, z, True).start()
         w_out(zo, 0).start()
         w_across(zn, 1).wait_recv()
-        w_across(zn, 0).wait_send()
+        w_across(z, 0, True).wait_send()
         w_across(zn, 1).start()
         for d in (2, 3):
             e_plane(d, z, True).start()
         acc2[...] = jnp.zeros_like(acc2)
         w_across(zf, 0).wait_recv()
-        w_out(zo, 0).wait_send()
+        w_out(z, 1).wait_send()
         w_out(zf, 0).start()
         spread(zn)
-        w_across(zn, 1).wait_send()
+        w_across(zn, 0).wait_send()
         e_chain(-outward, 1, zn).start()
+        e_chain(-outward, 1, z, True).start()
         w_across(z, 1).start()
         for d in (1, 2, 3):
             m_copy(d).wait_recv()
@@ -212,7 +211,7 @@
         for zp, xr in ((z, 0), (z, 1), (zn, 0), (zn, 1), (zo, 0), (zf, 0)):
             shrink(zp, xr, chunk)
         w_across(zf, 1).wait_recv()
-        w_out(zf, 0).wait_send()
+        w_out(zo, 0).wait_send()
         w_out(zf, 1).start()
         shrink(zf, 1, chunk)
         m2_copy().wait_recv()
@@ -223,26 +222,23 @@
         lax.fori_loop(1, nz, lambda i, c: (shrink_end((zo + i) % nz, 1), c)[1], 0)
         spread(zf)
         e_chain(outward, 0, zf).start()
-        w_across(z, 1).wait_send()
-        e_chain(-outward, 1, z, True).start()
+        spread(zo)
+        e_chain(outward, 0, zo).start()
         w_across(zo, 1).wait_recv()
-        w_out(zf, 1).wait_send()
+        w_out(zf, 0).wait_send()
         w_out(zo, 1).start()
         shrink_end(zo, 1)
         pbuf2[...] = acc2[...].astype(jnp.bfloat16)
         a_copy().start()
         shrink(zo, 1, chunk)
         send_partials()
-        spread(zo)
-        e_chain(outward, 0, zo).start()
 
     @pl.when(is_end)
     def _():
         zi, zf = z + inward, last - z
         zo = last - zi
+        w_in(z, 1).start()
         w_in(z, 0, True).wait_send()
-        w_in(z, 1).start()
-        w_in(z, 1).wait_send()
         e_chain(inward, 0, z, True).start()
         hi_copy(0).start()
         h_copy(1).wait_recv()
@@ -255,6 +251,7 @@
         for d in (2, 3):
             h_copy(d).wait_recv()
             hi_copy(d).start()
+        w_in(z, 1).wait_send()
         shrink(z, 0, lo)
         shrink(z, 1, lo)
         for xr in range(2):
@@ -265,12 +262,12 @@
             w_got(zp, xr).wait_recv()
             shrink(zp, xr, lo)
         spread(zf)
+        spread(zo)
         w_got(zo, 1).wait_recv()
         shrink(zo, 1, lo)
         a_copy().wait_recv()
         acc[...] += abuf[...].astype(jnp.float32)
         send_partials()
-        spread(zo)
 
     for copy in local_e:
         copy.wait()
@@ -307,6 +304,9 @@
         zf = last - zn
         a_copy().wait_send()
         w_out(zo, 1).wait_send()
+        w_out(zf, 1).wait_send()
+        w_across(zn, 1).wait_send()
+        w_across(z, 1).wait_send()
         for zp in (zo, zf):
             e_chain(outward, 0, zp).wait_send()
         e_chain(outward, 0, z, True).wait_send()

time: 53 us -> 52.8 us (level)
  no operation moved by 1% of the time
where the time goes in v4:
time: 52.8 us; the launch traced here: 52.7 us
  Pallas kernels  50.5 us (96%)
  other arithmetic  2.18 us (4%)
    pallas_call x1, Pallas kernels, local_planes(): pl.pallas_call(functools.partial(plane_kernel, nz), out_shape=(jax.ShapeD...  50.5 us
    convert_element_type x1, other arithmetic, local_planes(): (own.astype(jnp.float32) + peer_base.astype(jnp.float32) + delta).astype(...  2.18 us

profile of v4, /device:TPU:0, one launch (start us, length us, event | category | flops | bytes accessed | tf_op | source)
XLA Modules:
  0.0 52.7 jit_solution(14880634613657862619)
XLA Ops:
  0.0 0.0 copy-start
  0.0 50.5 %shard_map.55 = (f32[128,2,512]{2,1,0:T(2,128)}, bf16[128,2,512]{2,1,0:T(2,128)(2,1)}) custom-call(bf16[128,4096]{1,0:T(8,128)(2,1)} %hidden_ref.1, s32[1,128]{1,0:T(1,128)} %bitcast.4, bf16[1,4096,128]{2,1,0:T(8,128)(2,1)} %w_ref.1, bf16[1,2,64,512]{3,2,1,0:T(8,128)(2,1)} %e_ref.1, bf16[1,128,2,1024]{3,2,1,0:T(2,128)(2,1)} %base_ref.1), custom_call_target="tpu_custom_call" | custom-call | tf_op jit(solution)/shard_map/pallas_call | solution.py:345
  50.5 0.0 copy-done
  50.5 2.2 %fusion.1 = bf16[128,2,512]{2,1,0:T(2,128)(2,1)} fusion(f32[128,2,512]{2,1,0:T(2,128)} %get-tuple-element.8, bf16[128,2,512]{2,1,0:T(2,128)(2,1)} %get-tuple-element.7, bf16[1,128,2,1024]{3,2,1,0:T(2,128)(2,1)S(1)} %copy-done, s32[]{:T(128)S(6)} %select_n.3), kind=kLoop, calls=%fused_computation.2 | loop fusion | flops 655360 | bytes 1310724 | tf_op jit(solution)/shard_map/convert_element_type | solution.py:377
Async XLA Ops:
  0.0 50.5 %copy-start = (bf16[1,128,2,1024]{3,2,1,0:T(2,128)(2,1)S(1)}, bf16[1,128,2,1024]{3,2,1,0:T(2,128)(2,1)}, u32[]{:S(2)}) copy-start(bf16[1,128,2,1024]{3,2,1,0:T(2,128)(2,1)} %base_ref.1) | copy-start | bytes 1572868
